TPU v7x, 32 devices: a whole 2x2x4 slice. The times are simulated.
32 devices in a mesh: dp: 8 (over y, x, core), expert: 4 (over z).
Axes of the slice: x: 2, y: 2, z: 4, core: 2. Of those that a mesh axis runs over, the one named last changes fastest.
Arguments:
- hidden_in: bfloat16 [128, 4096], P(('dp', 'expert')), may hold values from -6 to 6
- norm_gain: bfloat16 [4096], replicated, may hold values from 0.099609375 to 1.8984375
- expert_ids: int32 [128, 8], P(('dp', 'expert')), may hold values from 0 to 63, all different within a row; in each aligned block of 16 rows (0 to 15, 16 to 31, ...) at most 4 rows name the same one
- gate_share: bfloat16 [128, 8], P(('dp', 'expert')), may hold values from 0.049804688 to 0.25
- w_gate: bfloat16 [512, 192, 4096], P(('dp', 'expert')), may hold values from -0.09375 to 0.09375
- w_up: bfloat16 [512, 192, 4096], P(('dp', 'expert')), may hold values from -0.09375 to 0.09375
- w_down: bfloat16 [512, 192, 4096], P(('dp', 'expert')), may hold values from -0.15625 to 0.15625
Outputs:
- layer_out: bfloat16 [128, 4096], P(('dp', 'expert'))
Inputs may be any that keep to these rules, and one draw needn't show every extreme that they name: `expert_ids`: each row names 8 different experts. Among the 16 rows of one request group (aligned blocks of 16 rows), no expert is named by more than 4 rows.
All inputs are finite; a program needn't handle non-finite values.
Results may differ from a plain program's by a relative error of at most 0.01.
Values may be sent and summed in bfloat16 or wider, within the bound.
A program may use at most 128 MiB of HBM per device.

v0:
```python
import jax
import jax.numpy as jnp
from jax import lax
from jax.sharding import PartitionSpec as P

EXPERTS = 64
SPLIT = 8


def body(hidden_in, norm_gain, expert_ids, gate_share, w_gate, w_up, w_down):
    dp_count = lax.axis_size("dp")
    col_count = lax.axis_size("expert")
    row_index = lax.axis_index("dp")
    column = lax.axis_index("expert")
    tok_dev = hidden_in.shape[0]
    model_width = hidden_in.shape[1]
    slot_dev = w_gate.shape[0]
    block_units = w_gate.shape[1]
    experts_row = EXPERTS // dp_count
    per_dev = max(1, slot_dev // SPLIT)
    runs_dev = slot_dev // per_dev
    capacity = tok_dev * col_count // 4
    resid = hidden_in.astype(jnp.float32)
    inv_rms = lax.rsqrt(jnp.mean(resid * resid, axis=1, keepdims=True) + 1e-06)
    normed = (resid * inv_rms * norm_gain.astype(jnp.float32)[None, :]).astype(jnp.bfloat16)
    row_x, row_share, row_ids = (
        lax.all_gather(normed, "expert", axis=0, tiled=True),
        lax.all_gather(gate_share, "expert", axis=0, tiled=True),
        lax.all_gather(expert_ids, "expert", axis=0, tiled=True),
    )
    tok_row = row_x.shape[0]
    flat_ids = row_ids.reshape(-1)
    onehot = (flat_ids[:, None] == jnp.arange(EXPERTS, dtype=jnp.int32)[None, :]).astype(jnp.int32)
    order_pos = jnp.sum((jnp.cumsum(onehot, axis=0) - onehot) * onehot, axis=1)
    slot_keys = (flat_ids * capacity + order_pos).reshape(tok_row, row_ids.shape[1])
    dest_rows = jnp.arange(dp_count, dtype=jnp.int32)[:, None]
    held = (dest_rows * col_count + column) * slot_dev // SPLIT + jnp.arange(
        per_dev, dtype=jnp.int32
    )[None, :]
    targets = held[:, :, None] * capacity + jnp.arange(capacity, dtype=jnp.int32)[None, None, :]
    matches = slot_keys[None, None, None, :, :] == targets[:, :, :, None, None]
    share_f = row_share.astype(jnp.float32)[None, None, None, :, :]
    weighted = jnp.sum(jnp.where(matches, share_f, 0.0), axis=4).astype(jnp.bfloat16)
    gate_w = w_gate.reshape(per_dev, runs_dev, block_units, model_width)
    up_w = w_up.reshape(per_dev, runs_dev, block_units, model_width)
    down_w = w_down.reshape(per_dev, runs_dev, block_units, model_width)
    part_rows = capacity // col_count
    row_experts = dest_rows * experts_row + jnp.arange(experts_row, dtype=jnp.int32)[None, :]
    section_targets = (
        row_experts[:, :, None] * capacity
        + column * part_rows
        + jnp.arange(part_rows, dtype=jnp.int32)[None, None, :]
    )
    section_hits = jnp.any(
        slot_keys[None, None, None, :, :] == section_targets[:, :, :, None, None], axis=4
    )
    section_blocks = jnp.einsum(
        "qmst,td->qmsd",
        section_hits.astype(jnp.bfloat16),
        row_x,
        preferred_element_type=jnp.float32,
    ).astype(jnp.bfloat16)
    landed = lax.all_to_all(section_blocks, "dp", split_axis=0, concat_axis=0, tiled=True)
    own_first = (row_index * col_count + column) * slot_dev // SPLIT - row_index * experts_row
    own_rows = lax.dynamic_slice_in_dim(
        lax.all_gather(landed, "expert", axis=2, tiled=True), own_first, per_dev, 1
    )
    gate_vals = jnp.einsum("qisd,igfd->qisgf", own_rows, gate_w, preferred_element_type=jnp.float32)
    up_vals = jnp.einsum("qisd,igfd->qisgf", own_rows, up_w, preferred_element_type=jnp.float32)
    activated = (jax.nn.silu(gate_vals) * up_vals).astype(jnp.bfloat16)
    projected = jnp.einsum(
        "qisgf,igfd->qisd", activated, down_w, preferred_element_type=jnp.float32
    )
    partial_value = projected.astype(jnp.bfloat16)
    returned = lax.all_to_all(partial_value, "dp", split_axis=0, concat_axis=0, tiled=True)
    routed = lax.psum_scatter(
        jnp.einsum("qist,qisd->td", weighted, returned, preferred_element_type=jnp.float32).astype(
            jnp.bfloat16
        ),
        "expert",
        scatter_dimension=0,
        tiled=True,
    ).astype(jnp.float32)
    return (resid + routed).astype(jnp.bfloat16)


def solution(mesh):
    placed = (
        P(("dp", "expert"), None),
        P(),
        P(("dp", "expert"), None),
        P(("dp", "expert"), None),
        P(("dp", "expert"), None, None),
        P(("dp", "expert"), None, None),
        P(("dp", "expert"), None, None),
    )
    return jax.shard_map(
        body, mesh=mesh, in_specs=placed, out_specs=P(("dp", "expert"), None), check_vma=False
    )
```

profile of v0, /device:TPU:0, one launch (start us, length us, event | category | flops | bytes accessed | tf_op | source)
XLA Modules:
  0.0 184.2 jit_solution(2676446387164438826)
XLA Ops:
  6.5 13.7 %all-gather = s32[4,4,8]{2,1,0:T(4,128)S(1)} all-gather(s32[1,4,8]{2,1,0:T(4,128)} %bitcast.70), channel_id=1, replica_groups=mesh['dp'=8,'expert'=4] {'expert'}, dimensions={0}, use_global_device_ids=true | all-gather | bytes 640 | tf_op jit(solution)/shard_map/all_gather | solution.py:29
  20.2 0.1 eq.49
  20.3 0.1 fusion.17
  20.4 0.2 reduce_window_sum.11
  20.6 0.2 select_reduce_fusion.1
  20.8 0.1 reduce_sum.30
  20.9 0.1 copy.15
  20.9 0.7 convert_element_type.47
  21.7 0.9 fusion.13
  22.6 0.8 fusion.18
  23.4 13.3 %all-gather.2 = bf16[4,4,4096]{2,1,0:T(4,128)(2,1)S(1)} all-gather(bf16[1,4,4096]{2,1,0:T(4,128)(2,1)S(1)} %fusion.18), channel_id=1, replica_groups=mesh['dp'=8,'expert'=4] {'expert'}, dimensions={0}, use_global_device_ids=true | all-gather | bytes 163840 | tf_op jit(solution)/shard_map/all_gather | solution.py:27
  36.8 0.1 multiply_add_fusion
  36.9 0.2 compare_reduce_fusion
  37.1 0.3 fusion.2
  37.3 13.4 %all_to_all.10 = bf16[8,8,1,4096]{3,1,2,0:T(8,128)(2,1)} all-to-all(bf16[8,8,1,4096]{3,1,2,0:T(8,128)(2,1)S(1)} %fusion.2), channel_id=1, replica_groups=mesh['dp'=8,'expert'=4] {'dp'}, dimensions={0} | all-to-all | bytes 1048576 | tf_op jit(solution)/shard_map/all_to_all | solution.py:63
  50.7 10.1 %all-gather.1 = bf16[4,4,8]{2,1,0:T(4,128)(2,1)S(1)} all-gather(bf16[1,4,8]{2,1,0:T(4,128)(2,1)} %bitcast.71), channel_id=1, replica_groups=mesh['dp'=8,'expert'=4] {'expert'}, dimensions={0}, use_global_device_ids=true | all-gather | bytes 320 | tf_op jit(solution)/shard_map/all_gather | solution.py:28
  60.8 0.1 copy.16
  60.9 33.9 %all-gather.5.cloned.1.call-done = bf16[8,8,4,4096]{3,1,0,2:T(8,128)(2,1)} async-done(((bf16[8,8,1,4096]{3,1,0,2:T(8,128)(2,1)}), bf16[8,8,4,4096]{3,1,0,2:T(8,128)(2,1)}) %all-gather.5.cloned.1.call-update) | async-done | bytes 2097168 | tf_op jit(solution)/shard_map/all_gather | solution.py:66
  94.7 2.2 %constant_dynamic-slice_fusion = bf16[8,2,4,4096]{3,1,0,2:T(2,128)(2,1)S(1)} fusion(bf16[8,8,4,4096]{3,1,0,2:T(8,128)(2,1)} %all-gather.5.cloned.1.call-done, s32[]{:T(128)S(6)} %select_n.25), kind=kLoop, calls=%fused_computation.43 | loop fusion | bytes 1048580 | tf_op jit(solution)/shard_map/dynamic_slice | solution.py:65
  97.0 12.4 %convolution_bitcast_fusion.3 = f32[8,2,4,8,192]{4,0,3,2,1:T(8,128)S(1)} fusion(bf16[2,8,192,4096,1]{3,2,1,4,0:T(8,128)(2,1)} %bitcast.72, bf16[8,2,4,4096]{3,1,0,2:T(2,128)(2,1)S(1)} %constant_dynamic-slice_fusion), kind=kOutput, calls=%fused_computation.8 | convolution fusion | flops 805306368 | bytes 26083328 | tf_op jit(solution)/shard_map/qisd,igfd->qisgf/dot_general | solution.py:68
  109.4 19.2 %fusion.1 = bf16[8,2,4,4096]{3,0,2,1:T(8,128)(2,1)S(1)} fusion(bf16[2,8,192,4096,1]{3,2,1,4,0:T(8,128)(2,1)} %bitcast.66, bf16[2,8,192,4096,1]{3,2,1,4,0:T(8,128)(2,1)} %bitcast.65, f32[8,2,4,8,192]{4,0,3,2,1:T(8,128)S(1)} %convolution_bitcast_fusion.3, bf16[8,2,4,4096]{3,1,0,2:T(2,128)(2,1)S(1)} %constant_dynamic-slice_fusion), kind=kOutput, calls=%fused_computation.3 | convolution fusion | flops 1611464704 | bytes 51773440 | tf_op jit(solution)/shard_map/qisgf,igfd->qisd/dot_general | solution.py:71
  128.6 1.2 copy.21
  129.8 3.6 %all-to-all-start.1 = ((bf16[8,2,4,4096]{3,2,1,0:T(4,128)(2,1)}), bf16[8,2,4,4096]{3,2,1,0:T(4,128)(2,1)S(1)}, u32[]{:S(2)}, u32[]{:S(2)}) async-start(bf16[8,2,4,4096]{3,2,1,0:T(4,128)(2,1)} %copy.21), calls=%async_computation.1 | async-start | bytes 1048576 | tf_op jit(solution)/shard_map/all_to_all | solution.py:75
  133.4 0.0 all-reduce.3.cloned.1.call-start
  133.5 0.1 add_multiply_fusion
  133.5 0.1 iota_add_fusion
  133.6 0.2 select_reduce_fusion
  133.8 9.4 %all-to-all-done.1 = bf16[8,2,4,4096]{3,2,1,0:T(4,128)(2,1)S(1)} async-done(((bf16[8,2,4,4096]{3,2,1,0:T(4,128)(2,1)}), bf16[8,2,4,4096]{3,2,1,0:T(4,128)(2,1)S(1)}, u32[]{:S(2)}, u32[]{:S(2)}) %all-to-all-start.1) | async-done | bytes 524320 | tf_op jit(solution)/shard_map/all_to_all | solution.py:75
  143.2 1.1 fusion.3
  144.3 0.6 dynamic-slice
  145.6 30.3 %all-reduce.3.cloned.1.call-done = bf16[16,4096]{1,0:T(8,128)(2,1)} async-done(((bf16[16,4096]{1,0:T(8,128)(2,1)}), bf16[16,4096]{1,0:T(8,128)(2,1)}) %all-reduce.3.cloned.1.call-update) | async-done | bytes 131088
  175.8 1.5 fusion.16
  (13 shorter events, 0.1 us)
Async XLA Ops:
  6.5 88.2 %all-gather.5.cloned.1.call-start = ((), (), s32[]{:S(2)}) async-start(), calls=%async_computation.2 | async-start | bytes 2621440 | tf_op jit(solution)/shard_map/all_gather | solution.py:66
  109.4 34.9 %copy-start.1 = (u32[32]{0:T(128)S(1)}, u32[32]{0:T(128)}, u32[]{:S(2)}) copy-start(u32[32]{0:T(128)} %constant.70) | copy-start | bytes 388
  109.4 66.5 %copy-start = (bf16[4,4096]{1,0:T(4,128)(2,1)S(1)}, bf16[4,4096]{1,0:T(4,128)(2,1)}, u32[]{:S(2)}) copy-start(bf16[4,4096]{1,0:T(4,128)(2,1)} %param.7) | copy-start | bytes 98308
  129.8 13.4 %all-to-all-start.1 = ((bf16[8,2,4,4096]{3,2,1,0:T(4,128)(2,1)}), bf16[8,2,4,4096]{3,2,1,0:T(4,128)(2,1)S(1)}, u32[]{:S(2)}, u32[]{:S(2)}) async-start(bf16[8,2,4,4096]{3,2,1,0:T(4,128)(2,1)} %copy.21), calls=%async_computation.1 | async-start | bytes 1048576 | tf_op jit(solution)/shard_map/all_to_all | solution.py:75
  133.4 42.4 %all-reduce.3.cloned.1.call-start = ((), (), s32[]{:S(2)}) async-start(), calls=%async_computation.3 | async-start | bytes 262144
Sparse Core Ops, SparseCore 0:
  50.8 43.8 all-gather.4
  144.4 31.3 all-reduce.2
where the time goes:
time: 185 us; the launch traced here: 184 us
  waiting for transfers between devices  73.6 us (40%)
  blocking collectives  50.4 us (27%)
  matrix products  32.9 us (18%)
  between operations  14.2 us (8%)
  other arithmetic  4.99 us (3%)
  local copies, waits for them, and re-layouts  4.38 us (2%)
  starting transfers between devices  3.68 us (2%)
    all_gather x1, waiting for transfers between devices, body(): lax.all_gather(landed, 'expert', axis=2, tiled=True)  33.9 us
    unnamed x3, waiting for transfers between devices  30.3 us
    dot_general x1, matrix products, body(): jnp.einsum('qisgf,igfd->qisd', activated, down_w, preferred_element_type=...  19.2 us
    all_gather x1, blocking collectives, body(): lax.all_gather(expert_ids, 'expert', axis=0, tiled=True)  13.7 us
    all_to_all x1, blocking collectives, body(): lax.all_to_all(section_blocks, 'dp', split_axis=0, concat_axis=0, tiled=T...  13.4 us
    all_gather x1, blocking collectives, body(): lax.all_gather(normed, 'expert', axis=0, tiled=True)  13.3 us
    dot_general x1, matrix products, body(): jnp.einsum('qisd,igfd->qisgf', own_rows, gate_w, preferred_element_type=j...  12.4 us
    all_gather x1, blocking collectives, body(): lax.all_gather(gate_share, 'expert', axis=0, tiled=True)  10.1 us
  transfers between devices with their start and end apart: 3, of which 3 were waited for; matrix products, arithmetic and copies ran while one was open for 1% of the time, Pallas kernels for 0%

commit v1 on v0

--- a/solution.py
+++ b/solution.py
@@ -1,13 +1,374 @@
+import functools
+
 import jax
 import jax.numpy as jnp
 from jax import lax
+from jax.experimental import pallas as pl
+from jax.experimental.pallas import tpu as pltpu
 from jax.sharding import PartitionSpec as P
 
 EXPERTS = 64
 SPLIT = 8
 
-
-def body(hidden_in, norm_gain, expert_ids, gate_share, w_gate, w_up, w_down):
+ROWS = 16
+QUART = 4
+META = 128
+PAIRS = 5
+MESH = pl.DeviceIdType.MESH
+BF = jnp.bfloat16
+F32 = jnp.float32
+
+
+def iota(shape, dim):
+    return lax.broadcasted_iota(jnp.int32, shape, dim)
+
+
+def dot(a, b):
+    return jnp.dot(a, b, preferred_element_type=F32)
+
+
+def dot_nt(a, b):
+    return lax.dot_general(a, b, (((1,), (1,)), ((), ())), preferred_element_type=F32)
+
+
+def tok_of(r):
+    return (r // ROWS) % QUART * 4 + r % 4
+
+
+def quarter_of(r):
+    return r % ROWS // 4
+
+
+def moe_kernel(
+    n_dp, n_z, n_exp, chunk, n_gu, n_j,
+    hid_ref, gain_ref, ids_ref, share_ref, wg, wu, wd,
+    out_ref,
+    buf, xs, gbuf, ubuf, dbuf, act, pay, ob_send, ob_recv, z_send, z_recv, z_own, fin, wmat,
+    g_sem, u_sem, d_sem,
+    zs_s, zs_r, xy_s, xy_r, co_s, co_r, fw_s, fw_r, ob_s, ob_r, zz_s, zz_r,
+):
+    dp = lax.axis_index("dp")
+    z = lax.axis_index("expert")
+    d_model = hid_ref.shape[1]
+    ff = n_gu * chunk
+    quarter = d_model // QUART
+    j_cols = d_model // n_j
+    j_quart = j_cols // QUART
+    cap_rows = n_dp * 4
+    n_rows = n_dp * n_z * ROWS
+
+    def gu_copies(p):
+        slot = lax.rem(p, PAIRS)
+        rows = pl.ds(pl.multiple_of(p * chunk, chunk), chunk)
+        return (
+            pltpu.make_async_copy(wg.at[rows], gbuf.at[slot], g_sem.at[slot]),
+            pltpu.make_async_copy(wu.at[rows], ubuf.at[slot], u_sem.at[slot]),
+        )
+
+    def d_copy(i, j):
+        return pltpu.make_async_copy(
+            wd.at[
+                pl.ds(pl.multiple_of(i * ff, ff), ff),
+                pl.ds(pl.multiple_of(j * j_cols, j_cols), j_cols),
+            ],
+            dbuf.at[j],
+            d_sem.at[j],
+        )
+
+    def start_gu(p):
+        a, b = gu_copies(p)
+        a.start()
+        b.start()
+
+    n_pairs = n_exp * n_gu
+    for p in range(n_gu):
+        start_gu(jnp.int32(p))
+    for j in range(n_j):
+        d_copy(jnp.int32(0), jnp.int32(j)).start()
+    for p in range(n_gu, min(PAIRS, n_pairs)):
+        start_gu(jnp.int32(p))
+
+    core = lax.rem(dp, 2)
+    xc = lax.rem(lax.div(dp, 2), 2)
+    yc = lax.div(dp, 4)
+    flip_c = 1 - 2 * core
+    flip_x = 2 - 4 * xc
+    flip_y = 4 - 8 * yc
+    sib = dp + flip_c
+    flips = (flip_x, flip_y, flip_x + flip_y)
+    barrier = pltpu.get_barrier_semaphore()
+    for k in range(1, n_dp):
+        pl.semaphore_signal(
+            barrier, inc=1, device_id=(lax.rem(dp + k, n_dp), z), device_id_type=MESH
+        )
+    for k in range(1, n_z):
+        pl.semaphore_signal(
+            barrier, inc=1, device_id=(dp, lax.rem(z + k, n_z)), device_id_type=MESH
+        )
+
+    resid = hid_ref[...].astype(F32)
+    inv_rms = lax.rsqrt(jnp.mean(resid * resid, axis=1, keepdims=True) + 1e-06)
+    normed = resid * inv_rms * gain_ref[...].astype(F32)
+    put = iota((8, META), 1) - iota((8, META), 0)
+    meta = dot(ids_ref[...].astype(F32).astype(BF), (put == 0).astype(F32).astype(BF)) + dot(
+        share_ref[...], (put == 8).astype(F32).astype(BF)
+    )
+    for j in range(QUART):
+        pay[4 * j : 4 * j + 4, 0:quarter] = normed[:, j * quarter : (j + 1) * quarter]
+        pay[4 * j : 4 * j + 4, quarter : quarter + META] = meta
+    me = dp * n_z + z
+    buf[me] = pay[...].astype(BF)
+
+    pl.semaphore_wait(barrier, n_dp - 1 + n_z - 1)
+
+    def remote(src, dst, s, r, to):
+        return pltpu.make_async_remote_copy(
+            src_ref=src, dst_ref=dst, send_sem=s, recv_sem=r, device_id=to, device_id_type=MESH
+        )
+
+    def z_copy(k):
+        blk = buf.at[me]
+        return remote(blk, blk, zs_s.at[k - 1], zs_r.at[k - 1], (dp, lax.rem(z + k, n_z)))
+
+    def xy_copy(f, k, zb):
+        blk = buf.at[dp * n_z + zb]
+        return remote(blk, blk, xy_s.at[f, k], xy_r.at[f, k], (dp + flips[f], z))
+
+    def co_copy(k, zb):
+        blk = buf.at[dp * n_z + zb]
+        return remote(blk, blk, co_s.at[k], co_r.at[k], (sib, z))
+
+    def fw_copy(f):
+        blk = buf.at[pl.ds((dp + flips[f]) * n_z, n_z)]
+        return remote(blk, blk, fw_s.at[f], fw_r.at[f], (sib, z))
+
+    for k in range(1, n_z):
+        z_copy(k).start()
+    for k in range(n_z):
+        zb = lax.rem(z + n_z - k, n_z)
+        if k > 0:
+            z_copy(k).wait_recv()
+        for f in range(3):
+            xy_copy(f, k, zb).start()
+        co_copy(k, zb).start()
+
+    tr, tc = iota((n_rows, 1), 0), iota((1, n_rows), 1)
+    before = (
+        (tr // (n_z * ROWS) == tc // (n_z * ROWS))
+        & (quarter_of(tr) == 0)
+        & (tok_of(tr) < tok_of(tc))
+    )
+    before = before.astype(F32).astype(BF)
+
+    for f in range(3):
+        for k in range(n_z):
+            xy_copy(f, k, z).wait_recv()
+        fw_copy(f).start()
+    for k in range(n_z):
+        co_copy(k, z).wait_recv()
+    for f in range(3):
+        fw_copy(f).wait_recv()
+
+    meta_all = buf[:, :, quarter : quarter + META].reshape(n_rows, META)
+    pick = (iota((16, META), 0) == iota((16, META), 1)).astype(F32).astype(BF)
+    meta_t = dot_nt(pick, meta_all)
+    ids_t = meta_t[0:8]
+    first = (me * n_exp).astype(F32)
+    lane_q = quarter_of(tc)
+    group = (tc // (n_z * ROWS) * 4).astype(F32)
+    slot_iota = iota((cap_rows, 1), 0).astype(F32)
+    for i in range(n_exp):
+        hit = jnp.sum((ids_t == first + i).astype(F32), axis=0, keepdims=True)
+        rank = dot(jnp.broadcast_to(hit, (8, n_rows)).astype(BF), before)[0:1]
+        key = jnp.where(hit > 0, group + rank, -1.0)
+        for j in range(QUART):
+            key_j = jnp.where(lane_q == j, key, -1.0)
+            sel = (slot_iota == key_j).astype(F32).astype(BF)
+            xs[i, :, j * quarter : (j + 1) * quarter] = dot(
+                sel, buf[:, :, 0:quarter].reshape(n_rows, quarter)
+            ).astype(BF)
+
+    grp = n_z * ROWS
+    meta_g = buf[pl.ds(dp * n_z, n_z), :, quarter : quarter + META].reshape(grp, META).astype(F32)
+    gr, gc = iota((grp, 1), 0), iota((1, grp), 1)
+    before_g = ((quarter_of(gc) == 0) & (tok_of(gc) < tok_of(gr))).astype(F32).astype(BF)
+    lanes = n_dp * ROWS
+    lc = iota((1, lanes), 1)
+    lane_first = ((lc // ROWS * n_z + z) * n_exp).astype(F32)
+    same_q = quarter_of(gr) == quarter_of(lc)
+    lane_slot = (lc % 4).astype(F32)
+    for i in range(n_exp):
+        hits = jnp.zeros((grp, lanes), F32)
+        shares = jnp.zeros((grp, lanes), F32)
+        for k in range(8):
+            match = meta_g[:, k : k + 1] == lane_first + i
+            hits = hits + match.astype(F32)
+            shares = shares + jnp.where(match, meta_g[:, 8 + k : 9 + k], 0.0)
+        rank = dot(before_g, hits.astype(BF))
+        keep = (hits > 0) & (rank == lane_slot) & same_q
+        wmat[i] = jnp.where(keep, shares, 0.0).astype(BF)
+
+    def ob_copy(i, j, k):
+        to = lax.rem(dp + k, n_dp)
+        return remote(
+            ob_send.at[i, j, to], ob_recv.at[i, j, dp], ob_s.at[i, j, k - 1],
+            ob_r.at[i, j, k - 1], (to, z),
+        )
+
+    pr, pc = iota((lanes, 1), 0), iota((1, cap_rows), 1)
+    same_slot = pr // ROWS * 4 + pr % 4 == pc
+    spread = [
+        (same_slot & (quarter_of(pr) == q)).astype(F32).astype(BF) for q in range(QUART)
+    ]
+
+    def expert(i, carry):
+        def gu_step(c, carry):
+            p = i * n_gu + c
+            slot = lax.rem(p, PAIRS)
+            a, b = gu_copies(p)
+            a.wait()
+            gate = dot_nt(xs[i], gbuf[slot])
+            b.wait()
+            up = dot_nt(xs[i], ubuf[slot])
+            act[c] = (gate / (1.0 + jnp.exp(-gate)) * up).astype(BF)
+
+            @pl.when(p + PAIRS < n_pairs)
+            def _():
+                start_gu(p + PAIRS)
+
+            return carry
+
+        lax.fori_loop(0, n_gu, gu_step, 0)
+
+        def d_step(j, carry):
+            d_copy(i, j).wait()
+            total = dot(act[0], dbuf[j, 0:chunk, :])
+            for c in range(1, n_gu):
+                total = total + dot(act[c], dbuf[j, c * chunk : (c + 1) * chunk, :])
+            total = total.astype(BF)
+
+            @pl.when(i + 1 < n_exp)
+            def _():
+                d_copy(i + 1, j).start()
+
+            rows = dot(spread[0], total[:, 0:j_quart])
+            for q in range(1, QUART):
+                rows = rows + dot(spread[q], total[:, q * j_quart : (q + 1) * j_quart])
+            ob_send[i, j] = rows.astype(BF).reshape(n_dp, ROWS, j_quart)
+            for k in range(1, n_dp):
+                ob_copy(i, j, k).start()
+            ob_recv[i, j, dp] = ob_send[i, j, dp]
+            return carry
+
+        lax.fori_loop(0, n_j, d_step, 0)
+        return carry
+
+    lax.fori_loop(0, n_exp, expert, 0)
+
+    def zz_copy(j, k):
+        to = lax.rem(z + k, n_z)
+        return remote(
+            z_send.at[j, to], z_recv.at[j, z], zz_s.at[j, k - 1], zz_r.at[j, k - 1], (dp, to)
+        )
+
+    for j in range(n_j):
+        part = jnp.zeros((grp, j_quart), F32)
+        for i in range(n_exp):
+            for k in range(1, n_dp):
+                ob_copy(i, j, k).wait_recv()
+            part = part + dot(wmat[i], ob_recv[i, j].reshape(lanes, j_quart))
+        z_send[j] = part.astype(BF).reshape(n_z, ROWS, j_quart)
+        z_own[j] = part.reshape(n_z, ROWS, j_quart)
+        for k in range(1, n_z):
+            zz_copy(j, k).start()
+    for j in range(n_j):
+        total = z_own[j, z]
+        for k in range(1, n_z):
+            zz_copy(j, k).wait_recv()
+            total = total + z_recv[j, lax.rem(z + n_z - k, n_z)].astype(F32)
+        fin[j] = total
+        for q in range(QUART):
+            at = j * j_cols + q * j_quart
+            out_ref[:, at : at + j_quart] = (
+                hid_ref[:, at : at + j_quart].astype(F32) + fin[j, 4 * q : 4 * q + 4, :]
+            ).astype(BF)
+
+    for k in range(1, n_z):
+        z_copy(k).wait_send()
+    for k in range(n_z):
+        for f in range(3):
+            xy_copy(f, k, z).wait_send()
+        co_copy(k, z).wait_send()
+    for f in range(3):
+        fw_copy(f).wait_send()
+    for j in range(n_j):
+        for i in range(n_exp):
+            for k in range(1, n_dp):
+                ob_copy(i, j, k).wait_send()
+        for k in range(1, n_z):
+            zz_copy(j, k).wait_send()
+
+
+def fused(hidden_in, norm_gain, expert_ids, gate_share, w_gate, w_up, w_down):
+    n_dp, n_z = lax.axis_size("dp"), lax.axis_size("expert")
+    tok, d_model = hidden_in.shape
+    slots, units, _ = w_gate.shape
+    n_exp = slots // SPLIT
+    ff = SPLIT * units
+    n_gu = 3
+    chunk = ff // n_gu
+    n_j = 4
+    j_cols = d_model // n_j
+    j_quart = j_cols // QUART
+    flat = (slots * units, d_model)
+    dma = pltpu.SemaphoreType.DMA
+    vmem = pl.BlockSpec(memory_space=pltpu.VMEM)
+    hbm = pl.BlockSpec(memory_space=pl.ANY)
+    wide = d_model // QUART + META
+    return pl.pallas_call(
+        functools.partial(moe_kernel, n_dp, n_z, n_exp, chunk, n_gu, n_j),
+        out_shape=jax.ShapeDtypeStruct((tok, d_model), BF),
+        in_specs=[vmem] * 4 + [hbm] * 3,
+        out_specs=vmem,
+        scratch_shapes=[
+            pltpu.VMEM((n_dp * n_z, ROWS, wide), BF),
+            pltpu.VMEM((n_exp, n_dp * 4, d_model), BF),
+            pltpu.VMEM((PAIRS, chunk, d_model), BF),
+            pltpu.VMEM((PAIRS, chunk, d_model), BF),
+            pltpu.VMEM((n_j, ff, j_cols), BF),
+            pltpu.VMEM((n_gu, n_dp * 4, chunk), BF),
+            pltpu.VMEM((ROWS, wide), F32),
+            pltpu.VMEM((n_exp, n_j, n_dp, ROWS, j_quart), BF),
+            pltpu.VMEM((n_exp, n_j, n_dp, ROWS, j_quart), BF),
+            pltpu.VMEM((n_j, n_z, ROWS, j_quart), BF),
+            pltpu.VMEM((n_j, n_z, ROWS, j_quart), BF),
+            pltpu.VMEM((n_j, n_z, ROWS, j_quart), F32),
+            pltpu.VMEM((n_j, ROWS, j_quart), F32),
+            pltpu.VMEM((n_exp, n_z * ROWS, n_dp * ROWS), BF),
+            dma((PAIRS,)), dma((PAIRS,)), dma((n_j,)),
+            dma((n_z - 1,)), dma((n_z - 1,)),
+            dma((3, n_z)), dma((3, n_z)),
+            dma((n_z,)), dma((n_z,)),
+            dma((3,)), dma((3,)),
+            dma((n_exp, n_j, n_dp - 1)), dma((n_exp, n_j, n_dp - 1)),
+            dma((n_j, n_z - 1)), dma((n_j, n_z - 1)),
+        ],
+        compiler_params=pltpu.CompilerParams(
+            collective_id=0, has_side_effects=True, vmem_limit_bytes=60 * 1024 * 1024
+        ),
+        cost_estimate=pl.CostEstimate(
+            flops=6 * slots * units * d_model * n_dp * 4,
+            bytes_accessed=6 * slots * units * d_model,
+            transcendentals=slots * units * n_dp * 4,
+        ),
+        name="routed_experts",
+    )(
+        hidden_in, norm_gain.reshape(1, d_model), expert_ids, gate_share,
+        w_gate.reshape(flat), w_up.reshape(flat), w_down.reshape(flat),
+    )
+
+
+def by_parts(hidden_in, norm_gain, expert_ids, gate_share, w_gate, w_up, w_down):
     dp_count = lax.axis_size("dp")
     col_count = lax.axis_size("expert")
     row_index = lax.axis_index("dp")
@@ -84,6 +445,14 @@
     return (resid + routed).astype(jnp.bfloat16)
 
 
+def body(hidden_in, norm_gain, expert_ids, gate_share, w_gate, w_up, w_down):
+    args = (hidden_in, norm_gain, expert_ids, gate_share, w_gate, w_up, w_down)
+    whole_experts = w_gate.shape[0] % SPLIT == 0
+    if whole_experts and lax.axis_size("dp") == 8 and lax.axis_size("expert") == 4:
+        return fused(*args)
+    return by_parts(*args)
+
+
 def solution(mesh):
     placed = (
         P(("dp", "expert"), None),

time: 185 us -> 54.2 us (0.29)
  waiting for transfers between devices: 73.6 us -> 0 us
  Pallas kernels: 0 us -> 51.2 us
  blocking collectives: 50.4 us -> 0 us
  matrix products: 32.9 us -> 0 us
  between operations: 14.2 us -> 0.01 us
  other arithmetic: 4.99 us -> 0 us
  starting transfers between devices: 3.68 us -> 0 us
    pallas_call x0 -> x1, Pallas kernels: none -> 51.2 us  [fused(): pl.pallas_call(functools.partial(moe_kernel, n_dp, n_z, n_exp, chunk, n_g...]
    all_gather x3 -> x0, blocking collectives: 37.1 us -> none  [the longest x1 13.7 us: body(): lax.all_gather(expert_ids, 'expert', axis=0, tiled=True)]
    all_gather x1 -> x0, waiting for transfers between devices: 33.9 us -> none  [body(): lax.all_gather(landed, 'expert', axis=2, tiled=True)]
    dot_general x4 -> x0, matrix products: 32.9 us -> none  [the longest x1 19.2 us: body(): jnp.einsum('qisgf,igfd->qisd', activated, down_w, preferred_element_type=...]
    unnamed x3 -> x0, waiting for transfers between devices: 30.3 us -> none
    all_to_all x1 -> x0, blocking collectives: 13.4 us -> none  [body(): lax.all_to_all(section_blocks, 'dp', split_axis=0, concat_axis=0, tiled=T...]
    all_to_all x1 -> x0, waiting for transfers between devices: 9.37 us -> none  [body(): lax.all_to_all(partial_value, 'dp', split_axis=0, concat_axis=0, tiled=True)]
    all_to_all x1 -> x0, starting transfers between devices: 3.64 us -> none  [body(): lax.all_to_all(partial_value, 'dp', split_axis=0, concat_axis=0, tiled=True)]
  transfers between devices with their start and end apart: 3 -> 0, of which waited for: 3 -> 0; matrix products, arithmetic and copies ran while one was open for 1% -> 0% of each run, Pallas kernels for 0% -> 0%
where the time goes in v1:
time: 54.2 us; the launch traced here: 54 us
  Pallas kernels  51.2 us (94%)
  local copies, waits for them, and re-layouts  2.7 us (5%)
    pallas_call x1, Pallas kernels, fused(): pl.pallas_call(functools.partial(moe_kernel, n_dp, n_z, n_exp, chunk, n_g...  51.2 us
    unnamed x1, local copies, waits for them, and re-layouts  1.39 us
    reshape x1, local copies, waits for them, and re-layouts, fused(): norm_gain.reshape(1, d_model)  1.31 us

profile of v1, /device:TPU:0, one launch (start us, length us, event | category | flops | bytes accessed | tf_op | source)
XLA Modules:
  0.0 54.0 jit_solution(16188934649916715715)
XLA Ops:
  0.0 1.3 %reshape.12.gain_ref = bf16[1,4096]{1,0:T(2,128)(2,1)} reshape(bf16[4096]{0:T(1024)(128)(2,1)} %param.8) | data formatting | bytes 16384 | tf_op jit(solution)/shard_map/reshape | solution.py:366
  1.3 51.2 %routed_experts.1 = bf16[4,4096]{1,0:T(4,128)(2,1)} custom-call(bf16[4,4096]{1,0:T(4,128)(2,1)} %hid_ref.1, bf16[1,4096]{1,0:T(2,128)(2,1)} %reshape.12.gain_ref, s32[4,8]{1,0:T(4,128)} %ids_ref.1, bf16[4,8]{1,0:T(4,128)(2,1)} %share_ref.1, bf16[3072,4096]{1,0:T(8,128)(2,1)} %bitcast.3, bf16[3072,4096]{1,0:T(8,128)(2,1)} %bitcast.4, bf16[3072,4096]{1,0:T(8,128)(2,1)} %bitcast.5), custom_call_target="tpu_custom_call" | custom-call | flops 2415919104 | bytes 75497472 | tf_op jit(solution)/shard_map/routed_experts/pallas_call | solution.py:328
  52.6 1.4 %copy.9 = bf16[4,4096]{1,0:T(4,128)(2,1)} copy(bf16[4,4096]{1,0:T(4,128)(2,1)} %routed_experts.1) | data formatting | bytes 65536

commit v2 on v1

--- a/solution.py
+++ b/solution.py
@@ -81,12 +81,19 @@
         b.start()
 
     n_pairs = n_exp * n_gu
+    first_copies = []
     for p in range(n_gu):
-        start_gu(jnp.int32(p))
-    for j in range(n_j):
-        d_copy(jnp.int32(0), jnp.int32(j)).start()
+        first_copies.extend(gu_copies(jnp.int32(p)))
+    first_copies.extend(d_copy(jnp.int32(0), jnp.int32(j)) for j in range(n_j))
     for p in range(n_gu, min(PAIRS, n_pairs)):
-        start_gu(jnp.int32(p))
+        first_copies.extend(gu_copies(jnp.int32(p)))
+    first_copies = iter(first_copies)
+
+    def stream(count):
+        for _, copy in zip(range(count), first_copies):
+            copy.start()
+
+    stream(2)
 
     core = lax.rem(dp, 2)
     xc = lax.rem(lax.div(dp, 2), 2)
@@ -108,7 +115,7 @@
 
     resid = hid_ref[...].astype(F32)
     inv_rms = lax.rsqrt(jnp.mean(resid * resid, axis=1, keepdims=True) + 1e-06)
-    normed = resid * inv_rms * gain_ref[...].astype(F32)
+    normed = resid * inv_rms * gain_ref[...].astype(F32).reshape(1, d_model)
     put = iota((8, META), 1) - iota((8, META), 0)
     meta = dot(ids_ref[...].astype(F32).astype(BF), (put == 0).astype(F32).astype(BF)) + dot(
         share_ref[...], (put == 8).astype(F32).astype(BF)
@@ -145,6 +152,8 @@
     for k in range(1, n_z):
         z_copy(k).start()
     for k in range(n_z):
+        if k > 0:
+            stream(1)
         zb = lax.rem(z + n_z - k, n_z)
         if k > 0:
             z_copy(k).wait_recv()
@@ -159,34 +168,7 @@
         & (tok_of(tr) < tok_of(tc))
     )
     before = before.astype(F32).astype(BF)
-
-    for f in range(3):
-        for k in range(n_z):
-            xy_copy(f, k, z).wait_recv()
-        fw_copy(f).start()
-    for k in range(n_z):
-        co_copy(k, z).wait_recv()
-    for f in range(3):
-        fw_copy(f).wait_recv()
-
-    meta_all = buf[:, :, quarter : quarter + META].reshape(n_rows, META)
-    pick = (iota((16, META), 0) == iota((16, META), 1)).astype(F32).astype(BF)
-    meta_t = dot_nt(pick, meta_all)
-    ids_t = meta_t[0:8]
-    first = (me * n_exp).astype(F32)
-    lane_q = quarter_of(tc)
-    group = (tc // (n_z * ROWS) * 4).astype(F32)
-    slot_iota = iota((cap_rows, 1), 0).astype(F32)
-    for i in range(n_exp):
-        hit = jnp.sum((ids_t == first + i).astype(F32), axis=0, keepdims=True)
-        rank = dot(jnp.broadcast_to(hit, (8, n_rows)).astype(BF), before)[0:1]
-        key = jnp.where(hit > 0, group + rank, -1.0)
-        for j in range(QUART):
-            key_j = jnp.where(lane_q == j, key, -1.0)
-            sel = (slot_iota == key_j).astype(F32).astype(BF)
-            xs[i, :, j * quarter : (j + 1) * quarter] = dot(
-                sel, buf[:, :, 0:quarter].reshape(n_rows, quarter)
-            ).astype(BF)
+    stream(2)
 
     grp = n_z * ROWS
     meta_g = buf[pl.ds(dp * n_z, n_z), :, quarter : quarter + META].reshape(grp, META).astype(F32)
@@ -207,6 +189,40 @@
         rank = dot(before_g, hits.astype(BF))
         keep = (hits > 0) & (rank == lane_slot) & same_q
         wmat[i] = jnp.where(keep, shares, 0.0).astype(BF)
+
+    for f in range(3):
+        for k in range(n_z):
+            xy_copy(f, k, z).wait_recv()
+        fw_copy(f).start()
+        stream(2)
+    for k in range(n_z):
+        co_copy(k, z).wait_recv()
+    for f in range(3):
+        fw_copy(f).wait_recv()
+    stream(n_pairs * 2 + n_j)
+
+    meta_all = buf[:, :, quarter : quarter + META].reshape(n_rows, META)
+    pick = (iota((16, META), 0) == iota((16, META), 1)).astype(F32).astype(BF)
+    meta_t = dot_nt(pick, meta_all)
+    ids_t = meta_t[0:8]
+    first = (me * n_exp).astype(F32)
+    lane_q = quarter_of(tc)
+    group = (tc // (n_z * ROWS) * 4).astype(F32)
+    slot_iota = iota((n_exp * cap_rows, 1), 0)
+    key = jnp.full((1, n_rows), -1.0, F32)
+    for i in range(n_exp):
+        hit = jnp.sum((ids_t == first + i).astype(F32), axis=0, keepdims=True)
+        rank = dot(jnp.broadcast_to(hit, (8, n_rows)).astype(BF), before)[0:1]
+        own_key = jnp.where(hit > 0, group + rank + i * cap_rows, -1.0)
+        key = jnp.where(slot_iota // cap_rows == i, own_key, key)
+    slot_f = slot_iota.astype(F32)
+    for j in range(QUART):
+        sel = ((slot_f == key) & (lane_q == j)).astype(F32).astype(BF)
+        xs[:, :, j * quarter : (j + 1) * quarter] = (
+            dot(sel, buf[:, :, 0:quarter].reshape(n_rows, quarter))
+            .astype(BF)
+            .reshape(n_exp, cap_rows, quarter)
+        )
 
     def ob_copy(i, j, k):
         to = lax.rem(dp + k, n_dp)
@@ -363,7 +379,7 @@
         ),
         name="routed_experts",
     )(
-        hidden_in, norm_gain.reshape(1, d_model), expert_ids, gate_share,
+        hidden_in, norm_gain, expert_ids, gate_share,
         w_gate.reshape(flat), w_up.reshape(flat), w_down.reshape(flat),
     )
 

time: 54.2 us -> 52.3 us (0.965)
  local copies, waits for them, and re-layouts: 2.7 us -> 1.39 us
  Pallas kernels: 51.2 us -> 50.6 us
    reshape x1 -> x0, local copies, waits for them, and re-layouts: 1.31 us -> none  [fused(): norm_gain.reshape(1, d_model)]
    pallas_call x1, Pallas kernels: 51.2 us -> 50.6 us  [fused(): pl.pallas_call(functools.partial(moe_kernel, n_dp, n_z, n_exp, chunk, n_g...]
where the time goes in v2:
time: 52.3 us; the launch traced here: 52 us
  Pallas kernels  50.6 us (97%)
  local copies, waits for them, and re-layouts  1.39 us (3%)
    pallas_call x1, Pallas kernels, fused(): pl.pallas_call(functools.partial(moe_kernel, n_dp, n_z, n_exp, chunk, n_g...  50.6 us
    unnamed x1, local copies, waits for them, and re-layouts  1.39 us

profile of v2, /device:TPU:0, one launch (start us, length us, event | category | flops | bytes accessed | tf_op | source)
XLA Modules:
  0.0 52.0 jit_solution(6567389606725158078)
XLA Ops:
  0.0 50.6 %routed_experts.1 = bf16[4,4096]{1,0:T(4,128)(2,1)} custom-call(bf16[4,4096]{1,0:T(4,128)(2,1)} %hid_ref.1, bf16[4096]{0:T(1024)(128)(2,1)} %gain_ref.1, s32[4,8]{1,0:T(4,128)} %ids_ref.1, bf16[4,8]{1,0:T(4,128)(2,1)} %share_ref.1, bf16[3072,4096]{1,0:T(8,128)(2,1)} %bitcast.3, bf16[3072,4096]{1,0:T(8,128)(2,1)} %bitcast.4, bf16[3072,4096]{1,0:T(8,128)(2,1)} %bitcast.5), custom_call_target="tpu_custom_call" | custom-call | flops 2415919104 | bytes 75497472 | tf_op jit(solution)/shard_map/routed_experts/pallas_call | solution.py:344
  50.6 1.4 %copy.9 = bf16[4,4096]{1,0:T(4,128)(2,1)} copy(bf16[4,4096]{1,0:T(4,128)(2,1)} %routed_experts.1) | data formatting | bytes 65536

commit v3 on v2

--- a/solution.py
+++ b/solution.py
@@ -13,7 +13,8 @@
 ROWS = 16
 QUART = 4
 META = 128
-PAIRS = 5
+WEIGHT_SLOTS = 9
+HALVES = 2
 MESH = pl.DeviceIdType.MESH
 BF = jnp.bfloat16
 F32 = jnp.float32
@@ -40,54 +41,48 @@
 
 
 def moe_kernel(
-    n_dp, n_z, n_exp, chunk, n_gu, n_j,
+    n_dp, n_z, n_exp, ff, n_j,
     hid_ref, gain_ref, ids_ref, share_ref, wg, wu, wd,
     out_ref,
-    buf, xs, gbuf, ubuf, dbuf, act, pay, ob_send, ob_recv, z_send, z_recv, z_own, fin, wmat,
-    g_sem, u_sem, d_sem,
-    zs_s, zs_r, xy_s, xy_r, co_s, co_r, fw_s, fw_r, ob_s, ob_r, zz_s, zz_r,
+    buf, meta_buf, xs, wbuf, acc_g, acc_u, act, pay, ob_send, ob_recv, z_send, z_recv, z_own,
+    fin, wmat,
+    w_sem,
+    zs_s, zs_r, xy_s, xy_r, co_s, co_r, fw_s, fw_r,
+    mz_s, mz_r, mxy_s, mxy_r, mco_s, mco_r, mfw_s, mfw_r,
+    ob_s, ob_r, zz_s, zz_r,
 ):
     dp = lax.axis_index("dp")
     z = lax.axis_index("expert")
     d_model = hid_ref.shape[1]
-    ff = n_gu * chunk
-    quarter = d_model // QUART
+    half = d_model // HALVES
+    quarter = half // QUART
     j_cols = d_model // n_j
     j_quart = j_cols // QUART
     cap_rows = n_dp * 4
     n_rows = n_dp * n_z * ROWS
 
-    def gu_copies(p):
-        slot = lax.rem(p, PAIRS)
-        rows = pl.ds(pl.multiple_of(p * chunk, chunk), chunk)
-        return (
-            pltpu.make_async_copy(wg.at[rows], gbuf.at[slot], g_sem.at[slot]),
-            pltpu.make_async_copy(wu.at[rows], ubuf.at[slot], u_sem.at[slot]),
+    n_head = 2 * n_exp
+
+    def w_copy(ref, i, h, n):
+        slot = lax.rem(n, WEIGHT_SLOTS)
+        return pltpu.make_async_copy(
+            ref.at[
+                pl.ds(pl.multiple_of(i * ff, ff), ff),
+                pl.ds(pl.multiple_of(h * half, half), half),
+            ],
+            wbuf.at[slot],
+            w_sem.at[slot],
         )
 
-    def d_copy(i, j):
-        return pltpu.make_async_copy(
-            wd.at[
-                pl.ds(pl.multiple_of(i * ff, ff), ff),
-                pl.ds(pl.multiple_of(j * j_cols, j_cols), j_cols),
-            ],
-            dbuf.at[j],
-            d_sem.at[j],
-        )
-
-    def start_gu(p):
-        a, b = gu_copies(p)
-        a.start()
-        b.start()
-
-    n_pairs = n_exp * n_gu
-    first_copies = []
-    for p in range(n_gu):
-        first_copies.extend(gu_copies(jnp.int32(p)))
-    first_copies.extend(d_copy(jnp.int32(0), jnp.int32(j)) for j in range(n_j))
-    for p in range(n_gu, min(PAIRS, n_pairs)):
-        first_copies.extend(gu_copies(jnp.int32(p)))
-    first_copies = iter(first_copies)
+    def chunk(n):
+        if n < n_head:
+            return w_copy((wg, wu)[n % 2], jnp.int32(n // 2), 0, jnp.int32(n))
+        i, at = divmod(n - n_head, 4)
+        ref, h = ((wg, 1), (wu, 1), (wd, 0), (wd, 1))[at]
+        return w_copy(ref, jnp.int32(i), h, jnp.int32(n))
+
+    n_chunks = n_head + 4 * n_exp
+    first_copies = iter([chunk(n) for n in range(min(WEIGHT_SLOTS, n_chunks))])
 
     def stream(count):
         for _, copy in zip(range(count), first_copies):
@@ -120,11 +115,15 @@
     meta = dot(ids_ref[...].astype(F32).astype(BF), (put == 0).astype(F32).astype(BF)) + dot(
         share_ref[...], (put == 8).astype(F32).astype(BF)
     )
-    for j in range(QUART):
-        pay[4 * j : 4 * j + 4, 0:quarter] = normed[:, j * quarter : (j + 1) * quarter]
-        pay[4 * j : 4 * j + 4, quarter : quarter + META] = meta
     me = dp * n_z + z
-    buf[me] = pay[...].astype(BF)
+    for h in range(HALVES):
+        for q in range(QUART):
+            at = h * half + q * quarter
+            pay[h, 4 * q : 4 * q + 4, 0:quarter] = normed[:, at : at + quarter]
+            if h == 0:
+                pay[0, 4 * q : 4 * q + 4, quarter : quarter + META] = meta
+    meta_buf[me] = pay[0].astype(BF)
+    buf[me] = pay[1, :, 0:quarter].astype(BF)
 
     pl.semaphore_wait(barrier, n_dp - 1 + n_z - 1)
 
@@ -133,33 +132,56 @@
             src_ref=src, dst_ref=dst, send_sem=s, recv_sem=r, device_id=to, device_id_type=MESH
         )
 
-    def z_copy(k):
-        blk = buf.at[me]
-        return remote(blk, blk, zs_s.at[k - 1], zs_r.at[k - 1], (dp, lax.rem(z + k, n_z)))
-
-    def xy_copy(f, k, zb):
-        blk = buf.at[dp * n_z + zb]
-        return remote(blk, blk, xy_s.at[f, k], xy_r.at[f, k], (dp + flips[f], z))
-
-    def co_copy(k, zb):
-        blk = buf.at[dp * n_z + zb]
-        return remote(blk, blk, co_s.at[k], co_r.at[k], (sib, z))
-
-    def fw_copy(f):
-        blk = buf.at[pl.ds((dp + flips[f]) * n_z, n_z)]
-        return remote(blk, blk, fw_s.at[f], fw_r.at[f], (sib, z))
-
-    for k in range(1, n_z):
-        z_copy(k).start()
-    for k in range(n_z):
-        if k > 0:
-            stream(1)
-        zb = lax.rem(z + n_z - k, n_z)
-        if k > 0:
-            z_copy(k).wait_recv()
+    held = (meta_buf, buf)
+    sems = (
+        (mz_s, mz_r, mxy_s, mxy_r, mco_s, mco_r, mfw_s, mfw_r),
+        (zs_s, zs_r, xy_s, xy_r, co_s, co_r, fw_s, fw_r),
+    )
+
+    def z_copy(h, k):
+        blk = held[h].at[me]
+        s, r = sems[h][0:2]
+        return remote(blk, blk, s.at[k - 1], r.at[k - 1], (dp, lax.rem(z + k, n_z)))
+
+    def xy_copy(h, f, k, zb):
+        blk = held[h].at[dp * n_z + zb]
+        s, r = sems[h][2:4]
+        return remote(blk, blk, s.at[f, k], r.at[f, k], (dp + flips[f], z))
+
+    def co_copy(h, k, zb):
+        blk = held[h].at[dp * n_z + zb]
+        s, r = sems[h][4:6]
+        return remote(blk, blk, s.at[k], r.at[k], (sib, z))
+
+    def fw_copy(h, f):
+        blk = held[h].at[pl.ds((dp + flips[f]) * n_z, n_z)]
+        s, r = sems[h][6:8]
+        return remote(blk, blk, s.at[f], r.at[f], (sib, z))
+
+    def forward(h):
         for f in range(3):
-            xy_copy(f, k, zb).start()
-        co_copy(k, zb).start()
+            for k in range(n_z):
+                xy_copy(h, f, k, z).wait_recv()
+            fw_copy(h, f).start()
+
+    def arrived(h):
+        for k in range(n_z):
+            co_copy(h, k, z).wait_recv()
+        for f in range(3):
+            fw_copy(h, f).wait_recv()
+
+    for h in range(HALVES):
+        for k in range(1, n_z):
+            z_copy(h, k).start()
+    for h in range(HALVES):
+        for k in range(n_z):
+            zb = lax.rem(z + n_z - k, n_z)
+            if k > 0:
+                z_copy(h, k).wait_recv()
+            for f in range(3):
+                xy_copy(h, f, k, zb).start()
+            co_copy(h, k, zb).start()
+        stream(2)
 
     tr, tc = iota((n_rows, 1), 0), iota((1, n_rows), 1)
     before = (
@@ -168,10 +190,14 @@
         & (tok_of(tr) < tok_of(tc))
     )
     before = before.astype(F32).astype(BF)
-    stream(2)
+
+    forward(0)
+    stream(WEIGHT_SLOTS)
 
     grp = n_z * ROWS
-    meta_g = buf[pl.ds(dp * n_z, n_z), :, quarter : quarter + META].reshape(grp, META).astype(F32)
+    meta_g = (
+        meta_buf[pl.ds(dp * n_z, n_z), :, quarter : quarter + META].reshape(grp, META).astype(F32)
+    )
     gr, gc = iota((grp, 1), 0), iota((1, grp), 1)
     before_g = ((quarter_of(gc) == 0) & (tok_of(gc) < tok_of(gr))).astype(F32).astype(BF)
     lanes = n_dp * ROWS
@@ -190,18 +216,9 @@
         keep = (hits > 0) & (rank == lane_slot) & same_q
         wmat[i] = jnp.where(keep, shares, 0.0).astype(BF)
 
-    for f in range(3):
-        for k in range(n_z):
-            xy_copy(f, k, z).wait_recv()
-        fw_copy(f).start()
-        stream(2)
-    for k in range(n_z):
-        co_copy(k, z).wait_recv()
-    for f in range(3):
-        fw_copy(f).wait_recv()
-    stream(n_pairs * 2 + n_j)
-
-    meta_all = buf[:, :, quarter : quarter + META].reshape(n_rows, META)
+    arrived(0)
+
+    meta_all = meta_buf[:, :, quarter : quarter + META].reshape(n_rows, META)
     pick = (iota((16, META), 0) == iota((16, META), 1)).astype(F32).astype(BF)
     meta_t = dot_nt(pick, meta_all)
     ids_t = meta_t[0:8]
@@ -215,14 +232,15 @@
         rank = dot(jnp.broadcast_to(hit, (8, n_rows)).astype(BF), before)[0:1]
         own_key = jnp.where(hit > 0, group + rank + i * cap_rows, -1.0)
         key = jnp.where(slot_iota // cap_rows == i, own_key, key)
-    slot_f = slot_iota.astype(F32)
-    for j in range(QUART):
-        sel = ((slot_f == key) & (lane_q == j)).astype(F32).astype(BF)
-        xs[:, :, j * quarter : (j + 1) * quarter] = (
-            dot(sel, buf[:, :, 0:quarter].reshape(n_rows, quarter))
-            .astype(BF)
-            .reshape(n_exp, cap_rows, quarter)
-        )
+    chosen = slot_iota.astype(F32) == key
+
+    def pick_rows(h):
+        for q in range(QUART):
+            sel = (chosen & (lane_q == q)).astype(F32).astype(BF)
+            rows = dot(sel, held[h][:, :, 0:quarter].reshape(n_rows, quarter)).astype(BF)
+            xs[h, :, :, q * quarter : (q + 1) * quarter] = rows.reshape(n_exp, cap_rows, quarter)
+
+    pick_rows(0)
 
     def ob_copy(i, j, k):
         to = lax.rem(dp + k, n_dp)
@@ -237,36 +255,44 @@
         (same_slot & (quarter_of(pr) == q)).astype(F32).astype(BF) for q in range(QUART)
     ]
 
+    def head(i, carry):
+        w_copy(wg, i, 0, 2 * i).wait()
+        acc_g[i] = dot_nt(xs[0, i], wbuf[2 * i])
+        w_copy(wu, i, 0, 2 * i + 1).wait()
+        acc_u[i] = dot_nt(xs[0, i], wbuf[2 * i + 1])
+
+        @pl.when(i == 0)
+        def _():
+            chunk(WEIGHT_SLOTS).start()
+            chunk(WEIGHT_SLOTS + 1).start()
+            forward(1)
+
+        return carry
+
+    lax.fori_loop(0, n_exp, head, 0)
+    chunk(WEIGHT_SLOTS + 2).start()
+    arrived(1)
+    pick_rows(1)
+
     def expert(i, carry):
-        def gu_step(c, carry):
-            p = i * n_gu + c
-            slot = lax.rem(p, PAIRS)
-            a, b = gu_copies(p)
-            a.wait()
-            gate = dot_nt(xs[i], gbuf[slot])
-            b.wait()
-            up = dot_nt(xs[i], ubuf[slot])
-            act[c] = (gate / (1.0 + jnp.exp(-gate)) * up).astype(BF)
-
-            @pl.when(p + PAIRS < n_pairs)
+        n = n_head + 4 * i
+        w_copy(wg, i, 1, n).wait()
+        gate = acc_g[i] + dot_nt(xs[1, i], wbuf[lax.rem(n, WEIGHT_SLOTS)])
+        gate = gate / (1.0 + jnp.exp(-gate))
+        w_copy(wu, i, 1, n + 1).wait()
+        up = acc_u[i] + dot_nt(xs[1, i], wbuf[lax.rem(n + 1, WEIGHT_SLOTS)])
+        act[...] = (gate * up).astype(BF)
+
+        def d_step(j, carry):
+            h = j // (n_j // HALVES)
+            slot = lax.rem(n + 2 + h, WEIGHT_SLOTS)
+            col = pl.multiple_of((j - h * (n_j // HALVES)) * j_cols, j_cols)
+
+            @pl.when(col == 0)
             def _():
-                start_gu(p + PAIRS)
-
-            return carry
-
-        lax.fori_loop(0, n_gu, gu_step, 0)
-
-        def d_step(j, carry):
-            d_copy(i, j).wait()
-            total = dot(act[0], dbuf[j, 0:chunk, :])
-            for c in range(1, n_gu):
-                total = total + dot(act[c], dbuf[j, c * chunk : (c + 1) * chunk, :])
-            total = total.astype(BF)
-
-            @pl.when(i + 1 < n_exp)
-            def _():
-                d_copy(i + 1, j).start()
-
+                w_copy(wd, i, h, n + 2 + h).wait()
+
+            total = dot(act[...], wbuf[slot, :, pl.ds(col, j_cols)]).astype(BF)
             rows = dot(spread[0], total[:, 0:j_quart])
             for q in range(1, QUART):
                 rows = rows + dot(spread[q], total[:, q * j_quart : (q + 1) * j_quart])
@@ -309,14 +335,15 @@
                 hid_ref[:, at : at + j_quart].astype(F32) + fin[j, 4 * q : 4 * q + 4, :]
             ).astype(BF)
 
-    for k in range(1, n_z):
-        z_copy(k).wait_send()
-    for k in range(n_z):
+    for h in range(HALVES):
+        for k in range(1, n_z):
+            z_copy(h, k).wait_send()
+        for k in range(n_z):
+            for f in range(3):
+                xy_copy(h, f, k, z).wait_send()
+            co_copy(h, k, z).wait_send()
         for f in range(3):
-            xy_copy(f, k, z).wait_send()
-        co_copy(k, z).wait_send()
-    for f in range(3):
-        fw_copy(f).wait_send()
+            fw_copy(h, f).wait_send()
     for j in range(n_j):
         for i in range(n_exp):
             for k in range(1, n_dp):
@@ -331,8 +358,6 @@
     slots, units, _ = w_gate.shape
     n_exp = slots // SPLIT
     ff = SPLIT * units
-    n_gu = 3
-    chunk = ff // n_gu
     n_j = 4
     j_cols = d_model // n_j
     j_quart = j_cols // QUART
@@ -340,20 +365,27 @@
     dma = pltpu.SemaphoreType.DMA
     vmem = pl.BlockSpec(memory_space=pltpu.VMEM)
     hbm = pl.BlockSpec(memory_space=pl.ANY)
-    wide = d_model // QUART + META
+    half = d_model // HALVES
+    quarter = half // QUART
+    gather_sems = [
+        dma(dims)
+        for dims in ((n_z - 1,), (3, n_z), (n_z,), (3,))
+        for _ in range(2)
+    ]
     return pl.pallas_call(
-        functools.partial(moe_kernel, n_dp, n_z, n_exp, chunk, n_gu, n_j),
+        functools.partial(moe_kernel, n_dp, n_z, n_exp, ff, n_j),
         out_shape=jax.ShapeDtypeStruct((tok, d_model), BF),
         in_specs=[vmem] * 4 + [hbm] * 3,
         out_specs=vmem,
         scratch_shapes=[
-            pltpu.VMEM((n_dp * n_z, ROWS, wide), BF),
-            pltpu.VMEM((n_exp, n_dp * 4, d_model), BF),
-            pltpu.VMEM((PAIRS, chunk, d_model), BF),
-            pltpu.VMEM((PAIRS, chunk, d_model), BF),
-            pltpu.VMEM((n_j, ff, j_cols), BF),
-            pltpu.VMEM((n_gu, n_dp * 4, chunk), BF),
-            pltpu.VMEM((ROWS, wide), F32),
+            pltpu.VMEM((n_dp * n_z, ROWS, quarter), BF),
+            pltpu.VMEM((n_dp * n_z, ROWS, quarter + META), BF),
+            pltpu.VMEM((HALVES, n_exp, n_dp * 4, half), BF),
+            pltpu.VMEM((WEIGHT_SLOTS, ff, half), BF),
+            pltpu.VMEM((n_exp, n_dp * 4, ff), F32),
+            pltpu.VMEM((n_exp, n_dp * 4, ff), F32),
+            pltpu.VMEM((n_dp * 4, ff), BF),
+            pltpu.VMEM((HALVES, ROWS, quarter + META), F32),
             pltpu.VMEM((n_exp, n_j, n_dp, ROWS, j_quart), BF),
             pltpu.VMEM((n_exp, n_j, n_dp, ROWS, j_quart), BF),
             pltpu.VMEM((n_j, n_z, ROWS, j_quart), BF),
@@ -361,11 +393,9 @@
             pltpu.VMEM((n_j, n_z, ROWS, j_quart), F32),
             pltpu.VMEM((n_j, ROWS, j_quart), F32),
             pltpu.VMEM((n_exp, n_z * ROWS, n_dp * ROWS), BF),
-            dma((PAIRS,)), dma((PAIRS,)), dma((n_j,)),
-            dma((n_z - 1,)), dma((n_z - 1,)),
-            dma((3, n_z)), dma((3, n_z)),
-            dma((n_z,)), dma((n_z,)),
-            dma((3,)), dma((3,)),
+            dma((WEIGHT_SLOTS,)),
+            *gather_sems,
+            *gather_sems,
             dma((n_exp, n_j, n_dp - 1)), dma((n_exp, n_j, n_dp - 1)),
             dma((n_j, n_z - 1)), dma((n_j, n_z - 1)),
         ],

time: 52.3 us -> 50.8 us (0.971)
  Pallas kernels: 50.6 us -> 49.1 us
    pallas_call x1, Pallas kernels: 50.6 us -> 49.1 us  [fused(): pl.pallas_call(functools.partial(moe_kernel, n_dp, n_z, n_exp, ff, n_j),...]
where the time goes in v3:
time: 50.8 us; the launch traced here: 50.5 us
  Pallas kernels  49.1 us (97%)
  local copies, waits for them, and re-layouts  1.39 us (3%)
    pallas_call x1, Pallas kernels, fused(): pl.pallas_call(functools.partial(moe_kernel, n_dp, n_z, n_exp, ff, n_j),...  49.1 us
    unnamed x1, local copies, waits for them, and re-layouts  1.39 us

profile of v3, /device:TPU:0, one launch (start us, length us, event | category | flops | bytes accessed | tf_op | source)
XLA Modules:
  0.0 50.5 jit_solution(4069216578541322057)
XLA Ops:
  0.0 49.1 %routed_experts.1 = bf16[4,4096]{1,0:T(4,128)(2,1)} custom-call(bf16[4,4096]{1,0:T(4,128)(2,1)} %hid_ref.1, bf16[4096]{0:T(1024)(128)(2,1)} %gain_ref.1, s32[4,8]{1,0:T(4,128)} %ids_ref.1, bf16[4,8]{1,0:T(4,128)(2,1)} %share_ref.1, bf16[3072,4096]{1,0:T(8,128)(2,1)} %bitcast.3, bf16[3072,4096]{1,0:T(8,128)(2,1)} %bitcast.4, bf16[3072,4096]{1,0:T(8,128)(2,1)} %bitcast.5), custom_call_target="tpu_custom_call" | custom-call | flops 2415919104 | bytes 75497472 | tf_op jit(solution)/shard_map/routed_experts/pallas_call | solution.py:375
  49.1 1.4 %copy.9 = bf16[4,4096]{1,0:T(4,128)(2,1)} copy(bf16[4,4096]{1,0:T(4,128)(2,1)} %routed_experts.1) | data formatting | bytes 65536

commit v4 on v3

--- a/solution.py
+++ b/solution.py
@@ -13,7 +13,7 @@
 ROWS = 16
 QUART = 4
 META = 128
-WEIGHT_SLOTS = 9
+WEIGHT_SLOTS = 8
 HALVES = 2
 MESH = pl.DeviceIdType.MESH
 BF = jnp.bfloat16
@@ -237,8 +237,11 @@
     def pick_rows(h):
         for q in range(QUART):
             sel = (chosen & (lane_q == q)).astype(F32).astype(BF)
-            rows = dot(sel, held[h][:, :, 0:quarter].reshape(n_rows, quarter)).astype(BF)
-            xs[h, :, :, q * quarter : (q + 1) * quarter] = rows.reshape(n_exp, cap_rows, quarter)
+            rows = dot(sel, held[h][:, :, 0:quarter].reshape(n_rows, quarter))
+            for i in range(n_exp):
+                xs[h, i, q * quarter : (q + 1) * quarter, :] = jnp.transpose(
+                    rows[i * cap_rows : (i + 1) * cap_rows]
+                ).astype(BF)
 
     pick_rows(0)
 
@@ -257,9 +260,9 @@
 
     def head(i, carry):
         w_copy(wg, i, 0, 2 * i).wait()
-        acc_g[i] = dot_nt(xs[0, i], wbuf[2 * i])
+        acc_g[i] = dot(wbuf[2 * i], xs[0, i])
         w_copy(wu, i, 0, 2 * i + 1).wait()
-        acc_u[i] = dot_nt(xs[0, i], wbuf[2 * i + 1])
+        acc_u[i] = dot(wbuf[2 * i + 1], xs[0, i])
 
         @pl.when(i == 0)
         def _():
@@ -271,17 +274,18 @@
 
     lax.fori_loop(0, n_exp, head, 0)
     chunk(WEIGHT_SLOTS + 2).start()
+    chunk(WEIGHT_SLOTS + 3).start()
     arrived(1)
     pick_rows(1)
 
     def expert(i, carry):
         n = n_head + 4 * i
         w_copy(wg, i, 1, n).wait()
-        gate = acc_g[i] + dot_nt(xs[1, i], wbuf[lax.rem(n, WEIGHT_SLOTS)])
+        gate = acc_g[i] + dot(wbuf[lax.rem(n, WEIGHT_SLOTS)], xs[1, i])
         gate = gate / (1.0 + jnp.exp(-gate))
         w_copy(wu, i, 1, n + 1).wait()
-        up = acc_u[i] + dot_nt(xs[1, i], wbuf[lax.rem(n + 1, WEIGHT_SLOTS)])
-        act[...] = (gate * up).astype(BF)
+        up = acc_u[i] + dot(wbuf[lax.rem(n + 1, WEIGHT_SLOTS)], xs[1, i])
+        act[...] = jnp.transpose(gate * up).astype(BF)
 
         def d_step(j, carry):
             h = j // (n_j // HALVES)
@@ -380,10 +384,10 @@
         scratch_shapes=[
             pltpu.VMEM((n_dp * n_z, ROWS, quarter), BF),
             pltpu.VMEM((n_dp * n_z, ROWS, quarter + META), BF),
-            pltpu.VMEM((HALVES, n_exp, n_dp * 4, half), BF),
+            pltpu.VMEM((HALVES, n_exp, half, n_dp * 4), BF),
             pltpu.VMEM((WEIGHT_SLOTS, ff, half), BF),
-            pltpu.VMEM((n_exp, n_dp * 4, ff), F32),
-            pltpu.VMEM((n_exp, n_dp * 4, ff), F32),
+            pltpu.VMEM((n_exp, ff, n_dp * 4), F32),
+            pltpu.VMEM((n_exp, ff, n_dp * 4), F32),
             pltpu.VMEM((n_dp * 4, ff), BF),
             pltpu.VMEM((HALVES, ROWS, quarter + META), F32),
             pltpu.VMEM((n_exp, n_j, n_dp, ROWS, j_quart), BF),

time: 50.8 us -> 56.4 us (1.11)
  Pallas kernels: 49.1 us -> 54.7 us
    pallas_call x1, Pallas kernels: 49.1 us -> 54.7 us  [fused(): pl.pallas_call(functools.partial(moe_kernel, n_dp, n_z, n_exp, ff, n_j),...]
where the time goes in v4:
time: 56.4 us; the launch traced here: 56.1 us
  Pallas kernels  54.7 us (97%)
  local copies, waits for them, and re-layouts  1.39 us (2%)
    pallas_call x1, Pallas kernels, fused(): pl.pallas_call(functools.partial(moe_kernel, n_dp, n_z, n_exp, ff, n_j),...  54.7 us
    unnamed x1, local copies, waits for them, and re-layouts  1.39 us

profile of v4, /device:TPU:0, one launch (start us, length us, event | category | flops | bytes accessed | tf_op | source)
XLA Modules:
  0.0 56.1 jit_solution(2430960317241337958)
XLA Ops:
  0.0 54.7 %routed_experts.1 = bf16[4,4096]{1,0:T(4,128)(2,1)} custom-call(bf16[4,4096]{1,0:T(4,128)(2,1)} %hid_ref.1, bf16[4096]{0:T(1024)(128)(2,1)} %gain_ref.1, s32[4,8]{1,0:T(4,128)} %ids_ref.1, bf16[4,8]{1,0:T(4,128)(2,1)} %share_ref.1, bf16[3072,4096]{1,0:T(8,128)(2,1)} %bitcast.3, bf16[3072,4096]{1,0:T(8,128)(2,1)} %bitcast.4, bf16[3072,4096]{1,0:T(8,128)(2,1)} %bitcast.5), custom_call_target="tpu_custom_call" | custom-call | flops 2415919104 | bytes 75497472 | tf_op jit(solution)/shard_map/routed_experts/pallas_call | solution.py:379
  54.7 1.4 %copy.9 = bf16[4,4096]{1,0:T(4,128)(2,1)} copy(bf16[4,4096]{1,0:T(4,128)(2,1)} %routed_experts.1) | data formatting | bytes 65536

commit v5 on v3

--- a/solution.py
+++ b/solution.py
@@ -14,6 +14,7 @@
 QUART = 4
 META = 128
 WEIGHT_SLOTS = 9
+TILE = 256
 HALVES = 2
 MESH = pl.DeviceIdType.MESH
 BF = jnp.bfloat16
@@ -255,11 +256,15 @@
         (same_slot & (quarter_of(pr) == q)).astype(F32).astype(BF) for q in range(QUART)
     ]
 
+    tiles = [slice(at, at + TILE) for at in range(0, ff, TILE)]
+
     def head(i, carry):
         w_copy(wg, i, 0, 2 * i).wait()
-        acc_g[i] = dot_nt(xs[0, i], wbuf[2 * i])
+        for t in tiles:
+            acc_g[i, :, t] = dot_nt(xs[0, i], wbuf[2 * i, t, :])
         w_copy(wu, i, 0, 2 * i + 1).wait()
-        acc_u[i] = dot_nt(xs[0, i], wbuf[2 * i + 1])
+        for t in tiles:
+            acc_u[i, :, t] = dot_nt(xs[0, i], wbuf[2 * i + 1, t, :])
 
         @pl.when(i == 0)
         def _():
@@ -277,11 +282,15 @@
     def expert(i, carry):
         n = n_head + 4 * i
         w_copy(wg, i, 1, n).wait()
-        gate = acc_g[i] + dot_nt(xs[1, i], wbuf[lax.rem(n, WEIGHT_SLOTS)])
-        gate = gate / (1.0 + jnp.exp(-gate))
+        slot = lax.rem(n, WEIGHT_SLOTS)
+        for t in tiles:
+            gate = acc_g[i, :, t] + dot_nt(xs[1, i], wbuf[slot, t, :])
+            acc_g[i, :, t] = gate / (1.0 + jnp.exp(-gate))
         w_copy(wu, i, 1, n + 1).wait()
-        up = acc_u[i] + dot_nt(xs[1, i], wbuf[lax.rem(n + 1, WEIGHT_SLOTS)])
-        act[...] = (gate * up).astype(BF)
+        slot_u = lax.rem(n + 1, WEIGHT_SLOTS)
+        for t in tiles:
+            up = acc_u[i, :, t] + dot_nt(xs[1, i], wbuf[slot_u, t, :])
+            act[:, t] = (acc_g[i, :, t] * up).astype(BF)
 
         def d_step(j, carry):
             h = j // (n_j // HALVES)
@@ -292,10 +301,11 @@
             def _():
                 w_copy(wd, i, h, n + 2 + h).wait()
 
-            total = dot(act[...], wbuf[slot, :, pl.ds(col, j_cols)]).astype(BF)
-            rows = dot(spread[0], total[:, 0:j_quart])
-            for q in range(1, QUART):
-                rows = rows + dot(spread[q], total[:, q * j_quart : (q + 1) * j_quart])
+            rows = jnp.zeros((lanes, j_quart), F32)
+            for q in range(QUART):
+                cols = pl.ds(pl.multiple_of(col + q * j_quart, j_quart), j_quart)
+                total = dot(act[...], wbuf[slot, :, cols]).astype(BF)
+                rows = rows + dot(spread[q], total)
             ob_send[i, j] = rows.astype(BF).reshape(n_dp, ROWS, j_quart)
             for k in range(1, n_dp):
                 ob_copy(i, j, k).start()

time: 50.8 us -> 53.7 us (1.057)
  Pallas kernels: 49.1 us -> 52 us
    pallas_call x1, Pallas kernels: 49.1 us -> 52 us  [fused(): pl.pallas_call(functools.partial(moe_kernel, n_dp, n_z, n_exp, ff, n_j),...]
where the time goes in v5:
time: 53.7 us; the launch traced here: 53.4 us
  Pallas kernels  52 us (97%)
  local copies, waits for them, and re-layouts  1.39 us (3%)
    pallas_call x1, Pallas kernels, fused(): pl.pallas_call(functools.partial(moe_kernel, n_dp, n_z, n_exp, ff, n_j),...  52 us
    unnamed x1, local copies, waits for them, and re-layouts  1.39 us

profile of v5, /device:TPU:0, one launch (start us, length us, event | category | flops | bytes accessed | tf_op | source)
XLA Modules:
  0.0 53.4 jit_solution(8707783852774195186)
XLA Ops:
  0.0 52.0 %routed_experts.1 = bf16[4,4096]{1,0:T(4,128)(2,1)} custom-call(bf16[4,4096]{1,0:T(4,128)(2,1)} %hid_ref.1, bf16[4096]{0:T(1024)(128)(2,1)} %gain_ref.1, s32[4,8]{1,0:T(4,128)} %ids_ref.1, bf16[4,8]{1,0:T(4,128)(2,1)} %share_ref.1, bf16[3072,4096]{1,0:T(8,128)(2,1)} %bitcast.3, bf16[3072,4096]{1,0:T(8,128)(2,1)} %bitcast.4, bf16[3072,4096]{1,0:T(8,128)(2,1)} %bitcast.5), custom_call_target="tpu_custom_call" | custom-call | flops 2415919104 | bytes 75497472 | tf_op jit(solution)/shard_map/routed_experts/pallas_call | solution.py:385
  52.1 1.4 %copy.9 = bf16[4,4096]{1,0:T(4,128)(2,1)} copy(bf16[4,4096]{1,0:T(4,128)(2,1)} %routed_experts.1) | data formatting | bytes 65536
